TPU v7x, 512 devices: a whole 4x4x16 slice. The times are simulated.
512 devices in a mesh: blk: 128 (over x, z, y_hi), feat: 4 (over y_lo, core).
Axes of the slice: x: 4, y: 4 (y_hi: 2, y_lo: 2; y = y_hi * 2 + y_lo), z: 16, core: 2. Of those that a mesh axis runs over, the one named last changes fastest.
Arguments:
- hidden_query: bfloat16 [65536, 4096], P('blk', 'feat'), may hold values from -6 to 6
- hidden_passage: bfloat16 [16384, 4096], P('blk', 'feat'), may hold values from -6 to 6
- embed_gain: float32 [4096], P('feat'), may hold values from 0.5 to 1.5
- positive: int32 [65536], P('blk'), may hold values from 0 to 16383, as said below
- tail_count: int32 [65536], P('blk'), may hold values from 769 to 896, as said below
Outputs:
- grad_query: float32 [65536, 4096], P('blk', 'feat')
- grad_passage: float32 [16384, 4096], P('blk', 'feat')
- grad_gain: float32 [4096], P('feat')
- loss: float32 [65536], P('blk')
Inputs may be any that keep to these rules, and one draw needn't show every extreme that they name: positive[q] lies in block q // 512 of the passages: from (q // 512) * 128 to (q // 512) * 128 + 127. Some query takes each end of the range of tail_count.
All inputs are finite; a program needn't handle non-finite values.
Results may differ from a plain program's by a relative error of at most 0.0041.
Values may be sent and summed in bfloat16 or wider, within the bound.
A program may use at most 64 MiB of HBM per device.

v0:
```python
import jax
import jax.numpy as jnp
from jax import lax
from jax.sharding import PartitionSpec as P

D = 4096
REACH = 3


margin = 1.0
loss_scale = 128.0


def passed_along(value, axis, steps):
    count = lax.axis_size(axis)
    pairs = [(source, (source + steps) % count) for source in range(count)]
    return lax.ppermute(value, axis, pairs)


def summed_scores(partial_value):
    return lax.psum(partial_value, "feat")


def shards(hidden_query, hidden_passage, embed_gain, positive, tail_count):
    blocks = lax.axis_size("blk")
    own_block = lax.axis_index("blk")
    rows_p = hidden_passage.shape[0]
    width = hidden_query.shape[1]
    score_scale = D ** (-0.5)
    queries = (hidden_query.astype(jnp.float32) * embed_gain).astype(jnp.bfloat16)
    passages = (hidden_passage.astype(jnp.float32) * embed_gain).astype(jnp.bfloat16)
    counts = tail_count.astype(jnp.float32)
    columns = jnp.arange(rows_p, dtype=jnp.int32)
    own_hot = columns[None, :] == (positive - own_block * rows_p)[:, None]

    def live_for(col_block):
        signed = (col_block - own_block + blocks // 2) % blocks - blocks // 2
        order = 2 * jnp.abs(signed) - jnp.where(signed > 0, 1, 0).astype(jnp.int32)
        rank = order * rows_p + columns
        global_col = col_block * rows_p + columns
        return (rank[None, :] < tail_count[:, None]) & (global_col[None, :] != positive[:, None])

    def terms(live, scores):
        weights = jnp.where(live, 1.0, 0.0).astype(jnp.float32)
        excess = scores - anchor[:, None] + margin
        loss_part = jnp.sum(weights * jax.nn.softplus(excess), axis=1) / counts
        grads = loss_scale * weights * jax.nn.sigmoid(excess) / counts[:, None]
        total_part = jnp.sum(grads, axis=1)
        grads_low = grads.astype(jnp.bfloat16)
        passage_part = (
            jnp.dot(grads_low.T, queries, preferred_element_type=jnp.float32) * score_scale
        )
        return (loss_part, total_part, grads_low, passage_part)

    own_scores = (
        summed_scores(jnp.dot(queries, passages.T, preferred_element_type=jnp.float32))
        * score_scale
    )
    anchor = jnp.sum(jnp.where(own_hot, own_scores, 0.0), axis=1)
    loss, row_total, own_grads, own_pass = terms(live_for(own_block), own_scores)
    grad_pieces = [own_grads]
    tile_pieces = [passages]
    tile = passed_along(passages, "blk", -REACH)
    moving = jnp.zeros((rows_p, width), jnp.float32)
    for step in range(2 * REACH + 1):
        if step == REACH:
            moving = moving + own_pass
        else:
            live = live_for((own_block + REACH - step) % blocks)
            scores = (
                summed_scores(jnp.dot(queries, tile.T, preferred_element_type=jnp.float32))
                * score_scale
            )
            loss_part, total_part, grads_low, passage_part = terms(live, scores)
            loss = loss + loss_part
            row_total = row_total + total_part
            moving = moving + passage_part
            grad_pieces.append(grads_low)
            tile_pieces.append(tile)
        if step < 2 * REACH:
            tile = passed_along(tile, "blk", 1)
            moving = passed_along(moving, "blk", 1)
    carried = passed_along(moving.astype(jnp.bfloat16), "blk", -REACH).astype(moving.dtype)
    dquery = (
        jnp.dot(
            jnp.concatenate(grad_pieces, axis=1),
            jnp.concatenate(tile_pieces, axis=0),
            preferred_element_type=jnp.float32,
        )
        * score_scale
    )
    pos_matrix = jnp.where(own_hot, -row_total[:, None], 0.0).astype(jnp.bfloat16)
    dquery = (
        dquery + jnp.dot(pos_matrix, passages, preferred_element_type=jnp.float32) * score_scale
    )
    dpassage = (
        carried + jnp.dot(pos_matrix.T, queries, preferred_element_type=jnp.float32) * score_scale
    )
    local_gain = jnp.sum(dquery * hidden_query.astype(jnp.float32), axis=0) + jnp.sum(
        dpassage * hidden_passage.astype(jnp.float32), axis=0
    )
    grad_gain = lax.psum(local_gain, "blk")
    return (dquery * embed_gain, dpassage * embed_gain, grad_gain, loss)


def solution(mesh):
    in_specs = (P("blk", "feat"), P("blk", "feat"), P("feat"), P("blk"), P("blk"))
    out_specs = (P("blk", "feat"), P("blk", "feat"), P("feat"), P("blk"))
    return jax.shard_map(shards, mesh=mesh, in_specs=in_specs, out_specs=out_specs, check_vma=False)
```

profile of v0, /device:TPU:8, one launch (start us, length us, event | category | flops | bytes accessed | tf_op | source)
XLA Modules:
  0.0 680.6 jit_solution(1155746480035557662)
XLA Ops:
  8.4 15.8 %collective-permute-start = (bf16[128,1024]{1,0:T(8,128)(2,1)S(1)}, bf16[128,1024]{1,0:T(8,128)(2,1)S(1)}, u32[]{:S(2)}, u32[]{:S(2)}) collective-permute-start(bf16[128,1024]{1,0:T(8,128)(2,1)S(1)} %get-tuple-element.19), channel_id=1, source_target_pairs={{0,500},{4,504},{8,508},{12,0},{16,4},{20,8},{24,12},{28,16},{32,2... | collective-permute-start | bytes 786440 | tf_op jit(solution)/shard_map/ppermute | solution.py:17
  24.2 11.1 %collective-permute-done = bf16[128,1024]{1,0:T(8,128)(2,1)S(1)} collective-permute-done((bf16[128,1024]{1,0:T(8,128)(2,1)S(1)}, bf16[128,1024]{1,0:T(8,128)(2,1)S(1)}, u32[]{:S(2)}, u32[]{:S(2)}) %collective-permute-start) | collective-permute-done | bytes 262176 | tf_op jit(solution)/shard_map/ppermute | solution.py:17
  37.2 2.4 fusion.64
  39.6 10.6 %collective-permute-done.1 = bf16[128,1024]{1,0:T(8,128)(2,1)S(1)} collective-permute-done((bf16[128,1024]{1,0:T(8,128)(2,1)S(1)}, bf16[128,1024]{1,0:T(8,128)(2,1)S(1)}, u32[]{:S(2)}, u32[]{:S(2)}) %collective-permute-start.1) | collective-permute-done | bytes 262176 | tf_op jit(solution)/shard_map/ppermute | solution.py:17
  53.2 10.9 %collective-permute-done.2 = bf16[128,1024]{1,0:T(8,128)(2,1)S(1)} collective-permute-done((bf16[128,1024]{1,0:T(8,128)(2,1)S(1)}, bf16[128,1024]{1,0:T(8,128)(2,1)S(1)}, u32[]{:S(2)}, u32[]{:S(2)}) %collective-permute-start.2) | collective-permute-done | bytes 262176 | tf_op jit(solution)/shard_map/ppermute | solution.py:17
  67.2 10.9 %collective-permute-done.3 = bf16[128,1024]{1,0:T(8,128)(2,1)S(1)} collective-permute-done((bf16[128,1024]{1,0:T(8,128)(2,1)S(1)}, bf16[128,1024]{1,0:T(8,128)(2,1)S(1)}, u32[]{:S(2)}, u32[]{:S(2)}) %collective-permute-start.3) | collective-permute-done | bytes 262176 | tf_op jit(solution)/shard_map/ppermute | solution.py:17
  81.2 10.9 %collective-permute-done.4 = bf16[128,1024]{1,0:T(8,128)(2,1)S(1)} collective-permute-done((bf16[128,1024]{1,0:T(8,128)(2,1)S(1)}, bf16[128,1024]{1,0:T(8,128)(2,1)S(1)}, u32[]{:S(2)}, u32[]{:S(2)}) %collective-permute-start.4) | collective-permute-done | bytes 262176 | tf_op jit(solution)/shard_map/ppermute | solution.py:17
  95.2 10.9 %collective-permute-done.5 = bf16[128,1024]{1,0:T(8,128)(2,1)S(1)} collective-permute-done((bf16[128,1024]{1,0:T(8,128)(2,1)S(1)}, bf16[128,1024]{1,0:T(8,128)(2,1)S(1)}, u32[]{:S(2)}, u32[]{:S(2)}) %collective-permute-start.5) | collective-permute-done | bytes 262176 | tf_op jit(solution)/shard_map/ppermute | solution.py:17
  109.2 10.9 %collective-permute-done.6 = bf16[128,1024]{1,0:T(8,128)(2,1)S(1)} collective-permute-done((bf16[128,1024]{1,0:T(8,128)(2,1)S(1)}, bf16[128,1024]{1,0:T(8,128)(2,1)S(1)}, u32[]{:S(2)}, u32[]{:S(2)}) %collective-permute-start.6) | collective-permute-done | bytes 262176 | tf_op jit(solution)/shard_map/ppermute | solution.py:17
  125.6 51.6 %all-reduce.3.cloned.1.call-done = (f32[512,128]{1,0:T(8,128)}, f32[512,128]{1,0:T(8,128)}, f32[512,128]{1,0:T(8,128)}, f32[512,128]{1,0:T(8,128)}, f32[512,128]...) async-done(((f32[512,128]{1,0:T(8,128)}, f32[512,128]{1,0:T(8,128)}, f32[512,128]{1,0:T(8,128)}, f32[512,128]{1,0:T(8,128)}, f32[512,128]{1,0:T(8,128)}, ...) | async-done | bytes 1835024 | tf_op jit(solution)/shard_map/psum | solution.py:21
  181.5 4.8 collective-permute-start.7
  187.9 16.5 %collective-permute-done.7 = f32[128,1024]{1,0:T(8,128)S(1)} collective-permute-done((f32[128,1024]{1,0:T(8,128)S(1)}, f32[128,1024]{1,0:T(8,128)S(1)}, u32[]{:S(2)}, u32[]{:S(2)}) %collective-permute-start.7) | collective-permute-done | bytes 524320 | tf_op jit(solution)/shard_map/ppermute | solution.py:17
  204.7 1.9 collective-permute-start.8
  208.0 18.0 %collective-permute-done.8 = f32[128,1024]{1,0:T(8,128)S(1)} collective-permute-done((f32[128,1024]{1,0:T(8,128)S(1)}, f32[128,1024]{1,0:T(8,128)S(1)}, u32[]{:S(2)}, u32[]{:S(2)}) %collective-permute-start.8) | collective-permute-done | bytes 524320 | tf_op jit(solution)/shard_map/ppermute | solution.py:17
  226.1 1.9 collective-permute-start.9
  230.8 15.6 %collective-permute-done.9 = f32[128,1024]{1,0:T(8,128)S(1)} collective-permute-done((f32[128,1024]{1,0:T(8,128)S(1)}, f32[128,1024]{1,0:T(8,128)S(1)}, u32[]{:S(2)}, u32[]{:S(2)}) %collective-permute-start.9) | collective-permute-done | bytes 524320 | tf_op jit(solution)/shard_map/ppermute | solution.py:17
  256.4 10.7 %collective-permute-done.10 = f32[128,1024]{1,0:T(8,128)} collective-permute-done((f32[128,1024]{1,0:T(8,128)}, f32[128,1024]{1,0:T(8,128)}, u32[]{:S(2)}, u32[]{:S(2)}) %collective-permute-start.10) | collective-permute-done | bytes 524320 | tf_op jit(solution)/shard_map/ppermute | solution.py:17
  268.2 2.2 collective-permute-start.11
  273.1 13.8 %collective-permute-done.11 = f32[128,1024]{1,0:T(8,128)S(1)} collective-permute-done((f32[128,1024]{1,0:T(8,128)S(1)}, f32[128,1024]{1,0:T(8,128)S(1)}, u32[]{:S(2)}, u32[]{:S(2)}) %collective-permute-start.11) | collective-permute-done | bytes 524320 | tf_op jit(solution)/shard_map/ppermute | solution.py:17
  286.9 1.9 collective-permute-start.12
  289.4 2.8 fusion.1
  292.2 12.3 %collective-permute-done.12 = f32[128,1024]{1,0:T(8,128)S(1)} collective-permute-done((f32[128,1024]{1,0:T(8,128)S(1)}, f32[128,1024]{1,0:T(8,128)S(1)}, u32[]{:S(2)}, u32[]{:S(2)}) %collective-permute-start.12) | collective-permute-done | bytes 524320 | tf_op jit(solution)/shard_map/ppermute | solution.py:17
  307.1 8.1 %collective-permute-done.13 = bf16[128,1024]{1,0:T(8,128)(2,1)S(1)} collective-permute-done((bf16[128,1024]{1,0:T(8,128)(2,1)S(1)}, bf16[128,1024]{1,0:T(8,128)(2,1)S(1)}, u32[]{:S(2)}, u32[]{:S(2)}) %collective-permute-start.13) | collective-permute-done | bytes 262176 | tf_op jit(solution)/shard_map/ppermute | solution.py:17
  316.1 357.6 %psum.63 = f32[1024]{0:T(1024)} all-reduce(f32[1024]{0:T(1024)S(1)} %add.460), channel_id=1, replica_groups=mesh['blk'=128,'feat'=4] {'blk'}, use_global_device_ids=true, to_apply=%region_17.18 | all-reduce | flops 1024 | bytes 8192 | tf_op jit(solution)/shard_map/psum | solution.py:102
  (192 shorter events, 51.3 us)
Async XLA Ops:
  7.2 170.0 %all-reduce.3.cloned.1.call-start = ((), (), s32[]{:S(2)}) async-start(), calls=%async_computation | async-start | bytes 3670016 | tf_op jit(solution)/shard_map/psum | solution.py:21
  8.4 113.6 %copy-start.7 = (bf16[128,1024]{1,0:T(8,128)(2,1)}, bf16[128,1024]{1,0:T(8,128)(2,1)S(1)}, u32[]{:S(2)}) copy-start(bf16[128,1024]{1,0:T(8,128)(2,1)S(1)} %get-tuple-element.19) | copy-start | bytes 786436
  8.4 26.9 %collective-permute-start = (bf16[128,1024]{1,0:T(8,128)(2,1)S(1)}, bf16[128,1024]{1,0:T(8,128)(2,1)S(1)}, u32[]{:S(2)}, u32[]{:S(2)}) collective-permute-start(bf16[128,1024]{1,0:T(8,128)(2,1)S(1)} %get-tuple-element.19), channel_id=1, source_target_pairs={{0,500},{4,504},{8,508},{12,0},{16,4},{20,8},{24,12},{28,16},{32,2... | collective-permute-start | bytes 786440 | tf_op jit(solution)/shard_map/ppermute | solution.py:17
  35.3 14.8 %collective-permute-start.1 = (bf16[128,1024]{1,0:T(8,128)(2,1)S(1)}, bf16[128,1024]{1,0:T(8,128)(2,1)S(1)}, u32[]{:S(2)}, u32[]{:S(2)}) collective-permute-start(bf16[128,1024]{1,0:T(8,128)(2,1)S(1)} %collective-permute-done), channel_id=1, source_target_pairs={{0,4},{4,8},{8,12},{12,16},{16,20},{20,24},{24,28},{28,32},{32,36}... | collective-permute-start | bytes 786440 | tf_op jit(solution)/shard_map/ppermute | solution.py:17
  50.2 14.0 %collective-permute-start.2 = (bf16[128,1024]{1,0:T(8,128)(2,1)S(1)}, bf16[128,1024]{1,0:T(8,128)(2,1)S(1)}, u32[]{:S(2)}, u32[]{:S(2)}) collective-permute-start(bf16[128,1024]{1,0:T(8,128)(2,1)S(1)} %collective-permute-done.1), channel_id=1, source_target_pairs={{0,4},{4,8},{8,12},{12,16},{16,20},{20,24},{24,28},{28,32},{32,36}... | collective-permute-start | bytes 786440 | tf_op jit(solution)/shard_map/ppermute | solution.py:17
  64.1 14.0 %collective-permute-start.3 = (bf16[128,1024]{1,0:T(8,128)(2,1)S(1)}, bf16[128,1024]{1,0:T(8,128)(2,1)S(1)}, u32[]{:S(2)}, u32[]{:S(2)}) collective-permute-start(bf16[128,1024]{1,0:T(8,128)(2,1)S(1)} %collective-permute-done.2), channel_id=1, source_target_pairs={{0,4},{4,8},{8,12},{12,16},{16,20},{20,24},{24,28},{28,32},{32,36}... | collective-permute-start | bytes 786440 | tf_op jit(solution)/shard_map/ppermute | solution.py:17
  78.1 14.0 %collective-permute-start.4 = (bf16[128,1024]{1,0:T(8,128)(2,1)S(1)}, bf16[128,1024]{1,0:T(8,128)(2,1)S(1)}, u32[]{:S(2)}, u32[]{:S(2)}) collective-permute-start(bf16[128,1024]{1,0:T(8,128)(2,1)S(1)} %collective-permute-done.3), channel_id=1, source_target_pairs={{0,4},{4,8},{8,12},{12,16},{16,20},{20,24},{24,28},{28,32},{32,36}... | collective-permute-start | bytes 786440 | tf_op jit(solution)/shard_map/ppermute | solution.py:17
  92.1 14.0 %collective-permute-start.5 = (bf16[128,1024]{1,0:T(8,128)(2,1)S(1)}, bf16[128,1024]{1,0:T(8,128)(2,1)S(1)}, u32[]{:S(2)}, u32[]{:S(2)}) collective-permute-start(bf16[128,1024]{1,0:T(8,128)(2,1)S(1)} %collective-permute-done.4), channel_id=1, source_target_pairs={{0,4},{4,8},{8,12},{12,16},{16,20},{20,24},{24,28},{28,32},{32,36}... | collective-permute-start | bytes 786440 | tf_op jit(solution)/shard_map/ppermute | solution.py:17
  106.1 14.0 %collective-permute-start.6 = (bf16[128,1024]{1,0:T(8,128)(2,1)S(1)}, bf16[128,1024]{1,0:T(8,128)(2,1)S(1)}, u32[]{:S(2)}, u32[]{:S(2)}) collective-permute-start(bf16[128,1024]{1,0:T(8,128)(2,1)S(1)} %collective-permute-done.5), channel_id=1, source_target_pairs={{0,4},{4,8},{8,12},{12,16},{16,20},{20,24},{24,28},{28,32},{32,36}... | collective-permute-start | bytes 786440 | tf_op jit(solution)/shard_map/ppermute | solution.py:17
  122.2 107.0 %copy-start.31 = (f32[512]{0:T(512)}, f32[512]{0:T(512)S(1)}, u32[]{:S(2)}) copy-start(f32[512]{0:T(512)S(1)} %convert_element_type.51) | copy-start | bytes 6148
  122.3 64.8 %copy-start.40 = (s32[128]{0:T(128)}, s32[128]{0:T(128)S(1)}, u32[]{:S(2)}) copy-start(s32[128]{0:T(128)S(1)} %get-tuple-element.40) | copy-start | bytes 1540
  122.3 84.4 %copy-start.44 = (s32[128]{0:T(128)}, s32[128]{0:T(128)S(1)}, u32[]{:S(2)}) copy-start(s32[128]{0:T(128)S(1)} %get-tuple-element.42) | copy-start | bytes 1540
  122.3 84.4 %copy-start.46 = (s32[128]{0:T(128)}, s32[128]{0:T(128)S(1)}, u32[]{:S(2)}) copy-start(s32[128]{0:T(128)S(1)} %get-tuple-element.43) | copy-start | bytes 1540
  122.3 84.8 %copy-start.48 = (s32[128]{0:T(128)}, s32[128]{0:T(128)S(1)}, u32[]{:S(2)}) copy-start(s32[128]{0:T(128)S(1)} %get-tuple-element.44) | copy-start | bytes 1540
  122.4 84.8 %copy-start.50 = (s32[128]{0:T(128)}, s32[128]{0:T(128)S(1)}, u32[]{:S(2)}) copy-start(s32[128]{0:T(128)S(1)} %get-tuple-element.45) | copy-start | bytes 1540
  122.4 106.8 %copy-start.52 = (s32[128]{0:T(128)}, s32[128]{0:T(128)S(1)}, u32[]{:S(2)}) copy-start(s32[128]{0:T(128)S(1)} %get-tuple-element.46) | copy-start | bytes 1540
  122.4 106.8 %copy-start.54 = (s32[128]{0:T(128)}, s32[128]{0:T(128)S(1)}, u32[]{:S(2)}) copy-start(s32[128]{0:T(128)S(1)} %get-tuple-element.47) | copy-start | bytes 1540
  181.5 22.8 %collective-permute-start.7 = (f32[128,1024]{1,0:T(8,128)S(1)}, f32[128,1024]{1,0:T(8,128)S(1)}, u32[]{:S(2)}, u32[]{:S(2)}) collective-permute-start(f32[128,1024]{1,0:T(8,128)S(1)} %convolution_multiply_fusion.7), channel_id=1, source_target_pairs={{0,4},{4,8},{8,12},{12,16},{16,20},{20,24},{24,28},{28,32},{32,36}... | collective-permute-start | bytes 1572872 | tf_op jit(solution)/shard_map/ppermute | solution.py:17
  204.7 21.2 %collective-permute-start.8 = (f32[128,1024]{1,0:T(8,128)S(1)}, f32[128,1024]{1,0:T(8,128)S(1)}, u32[]{:S(2)}, u32[]{:S(2)}) collective-permute-start(f32[128,1024]{1,0:T(8,128)S(1)} %fusion.2), channel_id=1, source_target_pairs={{0,4},{4,8},{8,12},{12,16},{16,20},{20,24},{24,28},{28,32},{32,36}... | collective-permute-start | bytes 1572872 | tf_op jit(solution)/shard_map/ppermute | solution.py:17
  226.1 20.4 %collective-permute-start.9 = (f32[128,1024]{1,0:T(8,128)S(1)}, f32[128,1024]{1,0:T(8,128)S(1)}, u32[]{:S(2)}, u32[]{:S(2)}) collective-permute-start(f32[128,1024]{1,0:T(8,128)S(1)} %add.453), channel_id=1, source_target_pairs={{0,4},{4,8},{8,12},{12,16},{16,20},{20,24},{24,28},{28,32},{32,36}... | collective-permute-start | bytes 1572872 | tf_op jit(solution)/shard_map/ppermute | solution.py:17
  247.3 19.8 %collective-permute-start.10 = (f32[128,1024]{1,0:T(8,128)}, f32[128,1024]{1,0:T(8,128)}, u32[]{:S(2)}, u32[]{:S(2)}) collective-permute-start(f32[128,1024]{1,0:T(8,128)} %add.454), channel_id=1, source_target_pairs={{0,4},{4,8},{8,12},{12,16},{16,20},{20,24},{24,28},{28,32},{32,36}... | collective-permute-start | bytes 1572872 | tf_op jit(solution)/shard_map/ppermute | solution.py:17
  268.2 18.7 %collective-permute-start.11 = (f32[128,1024]{1,0:T(8,128)S(1)}, f32[128,1024]{1,0:T(8,128)S(1)}, u32[]{:S(2)}, u32[]{:S(2)}) collective-permute-start(f32[128,1024]{1,0:T(8,128)S(1)} %add.455), channel_id=1, source_target_pairs={{0,4},{4,8},{8,12},{12,16},{16,20},{20,24},{24,28},{28,32},{32,36}... | collective-permute-start | bytes 1572872 | tf_op jit(solution)/shard_map/ppermute | solution.py:17
  286.9 17.6 %collective-permute-start.12 = (f32[128,1024]{1,0:T(8,128)S(1)}, f32[128,1024]{1,0:T(8,128)S(1)}, u32[]{:S(2)}, u32[]{:S(2)}) collective-permute-start(f32[128,1024]{1,0:T(8,128)S(1)} %add.456), channel_id=1, source_target_pairs={{0,4},{4,8},{8,12},{12,16},{16,20},{20,24},{24,28},{28,32},{32,36}... | collective-permute-start | bytes 1572872 | tf_op jit(solution)/shard_map/ppermute | solution.py:17
  304.6 10.7 %collective-permute-start.13 = (bf16[128,1024]{1,0:T(8,128)(2,1)S(1)}, bf16[128,1024]{1,0:T(8,128)(2,1)S(1)}, u32[]{:S(2)}, u32[]{:S(2)}) collective-permute-start(bf16[128,1024]{1,0:T(8,128)(2,1)S(1)} %add_convert_fusion), channel_id=1, source_target_pairs={{0,500},{4,504},{8,508},{12,0},{16,4},{20,8},{24,12},{28,16},{32,2... | collective-permute-start | bytes 786440 | tf_op jit(solution)/shard_map/ppermute | solution.py:17
  (53 other events, 1243.7 us)
Sparse Core Ops, SparseCore 0:
  122.1 55.1 all-reduce.2
where the time goes:
time: 681 us
  blocking collectives  358 us (53%)
  waiting for transfers between devices  223 us (33%)
  starting transfers between devices  43.9 us (6%)
  other arithmetic  19.2 us (3%)
  matrix products  18.3 us (3%)
  between operations  15.4 us (2%)
    psum x1, blocking collectives, shards(): grad_gain = lax.psum(local_gain, 'blk')  358 us
    ppermute x14, waiting for transfers between devices, passed_along(): return lax.ppermute(value, axis, pairs)  171 us
    psum x1, waiting for transfers between devices, summed_scores(): return lax.psum(partial_value, 'feat')  51.6 us
    ppermute x14, starting transfers between devices, passed_along(): return lax.ppermute(value, axis, pairs)  43.8 us
  transfers between devices with their start and end apart: 15, of which 15 were waited for; matrix products, arithmetic and copies ran while one was open for 4% of the time, Pallas kernels for 0%

commit v1 on v0

v1 whole, which is shorter than its diff:
```python
import jax
import jax.numpy as jnp
from jax import lax
from jax.experimental import pallas as pl
from jax.experimental.pallas import tpu as pltpu
from jax.sharding import PartitionSpec as P

MESH = pl.DeviceIdType.MESH
MARGIN = 1.0
LOSS_SCALE = 128.0
D = 4096
SCALE = D ** (-0.5)
N_BLK = 128
NZ = 16
NXY = 8
PB = 128
QB = 512
HALF = 256
WIDTH = 1024

OWN, R, F, K, FR, KR, FAR = range(7)
OFFSET = {OWN: 0, R: 1, F: 2, K: -2, FR: 3, KR: -1, FAR: -3}
ROLES = (R, F, K, FR, KR, FAR)

ORDER = (
    "S0", "r0", "H0", "r1", "S1", "S2", "H1", "S3", "H2", "H3", "k0", "G1", "G2", "k1", "S5", "G3",
    "D2", "D3", "S4", "H5", "H4", "D1", "S6", "G5", "G4", "H6", "D5", "D4", "G6", "G0",
    "D6", "D0", "Q", "N", "M", "Z", "X",
)
FC = 2
RC = 4
CHAIN = True


def kernel(
    hq_hbm, hp_hbm, gain_hbm, pos_hbm, tail_hbm,
    gq_hbm, gp_hbm, gg_ref, loss_ref,
    hq, gain_ref, pos_ref, tail_ref, hpt, q, p, sx, rx, hb, hr, gt, rpart, kpart, ret_out, ret_in, dq, dp, zbuf, xbuf, lbuf,
    local_sem, out_sem, fwd_send, fwd_recv, x1_send, x1_recv, x2_send, x2_recv,
    x3_send, x3_recv, ret_send, ret_recv, z_send, z_recv, xy_send, xy_recv, loss_send, loss_recv,
):
    b = lax.axis_index("blk")
    f = lax.axis_index("feat")
    h = lax.rem(b, 2)
    x = b // 32
    z = lax.rem(b, 32) // 2
    core = lax.rem(f, 2)
    sigma = 1 - 2 * h

    def block_at(role):
        return lax.rem(b + N_BLK + sigma * OFFSET[role], N_BLK)

    def dev(role):
        return (block_at(role), f)

    mate = (b, f + 1 - 2 * core)
    across = (b, lax.rem(f + 2, 4))

    def z_peer(k):
        return (x * 32 + lax.rem(z + k, NZ) * 2 + h, f)

    place = x * 2 + h

    def xy_peer(k):
        e = lax.rem(place + k, NXY)
        return ((e // 2) * 32 + z * 2 + lax.rem(e, 2), f)

    load_hp = pltpu.make_async_copy(hp_hbm, hpt.at[OWN], local_sem.at[0])
    load_hq = pltpu.make_async_copy(hq_hbm, hq, local_sem.at[1])
    small = [
        pltpu.make_async_copy(src, dst, local_sem.at[2 + i])
        for i, (src, dst) in enumerate(
            ((gain_hbm, gain_ref), (pos_hbm, pos_ref), (tail_hbm, tail_ref))
        )
    ]
    for copy in [load_hp, load_hq] + small:
        copy.start()

    peers = [dev(r) for r in ROLES] + [mate, across]
    peers += [z_peer(k) for k in range(1, NZ)] + [xy_peer(k) for k in range(1, NXY)]
    barrier = pltpu.get_barrier_semaphore()
    for peer in peers:
        pl.semaphore_signal(barrier, inc=1, device_id=peer, device_id_type=MESH)
    pl.semaphore_wait(barrier, len(peers))

    sends = []

    def send(src, dst, s_sem, r_sem, to):
        copy = pltpu.make_async_remote_copy(
            src_ref=src, dst_ref=dst, send_sem=s_sem, recv_sem=r_sem,
            device_id=to, device_id_type=MESH,
        )
        copy.start()
        sends.append(copy)
        return copy

    def forward(src, slot, i, to):
        rows = pl.ds(i * (PB // FC), PB // FC)
        return send(
            src.at[rows, :], hpt.at[slot, rows, :], fwd_send.at[slot, i], fwd_recv.at[slot, i], dev(to)
        )

    fwd = {}
    for i in range(FC):
        fwd[R, i] = forward(hp_hbm, R, i, R)
    for i in range(FC):
        fwd[K, i] = forward(hp_hbm, K, i, F)
        fwd[F, i] = forward(hp_hbm, F, i, K)

    for copy in small:
        copy.wait()
    gain = gain_ref[...]
    pos_rows = [pos_ref[pl.ds(i, 1), :] for i in range(4)]
    pos_all = jnp.concatenate(pos_rows, axis=1) - b * PB
    pos_half = (
        jnp.concatenate([pos_ref[pl.ds(2 * core, 1), :], pos_ref[pl.ds(2 * core + 1, 1), :]], axis=1)
        - b * PB
    )
    tail_half = jnp.concatenate(
        [tail_ref[pl.ds(2 * core, 1), :], tail_ref[pl.ds(2 * core + 1, 1), :]], axis=1
    )
    count_half = tail_half.astype(jnp.float32)
    col_half = lax.broadcasted_iota(jnp.int32, (PB, HALF), 0)

    x1, x2, x3, ret = {}, {}, {}, {}
    state = {"anchor": None, "loss": 0.0, "total": 0.0, "gain": 0.0}

    load_hq.wait()
    q[...] = (hq[...].astype(jnp.float32) * gain).astype(jnp.bfloat16)
    load_hp.wait()

    def relay_r(i):
        fwd[R, i].wait_recv()
        fwd[KR, i] = forward(hpt.at[R], KR, i, F)
        fwd[FR, i] = forward(hpt.at[R], FR, i, K)

    def relay_k(i):
        fwd[KR, i].wait_recv()
        fwd[FAR, i] = forward(hpt.at[KR], FAR, i, F)

    def stage_s(t):
        if t in (F, K, FR, FAR):
            for i in range(FC):
                fwd[t, i].wait_recv()
        rows = pl.ds(t * PB, PB)
        tile = (hpt[t].astype(jnp.float32) * gain).astype(jnp.bfloat16)
        p[rows, :] = tile
        s = lax.dot_general(
            tile, q[...], (((1,), (1,)), ((), ())), preferred_element_type=jnp.float32
        ) * SCALE
        if t == OWN:
            hot = lax.broadcasted_iota(jnp.int32, (PB, QB), 0) == pos_all
            state["anchor"] = jnp.sum(jnp.where(hot, s, 0.0), axis=0, keepdims=True)
        s = s - state["anchor"]
        sx[t, 0] = s[:, :HALF]
        sx[t, 1] = s[:, HALF:]
        x1[t] = send(sx.at[t, 1 - core], rx.at[t], x1_send.at[t], x1_recv.at[t], mate)

    def stage_h(t):
        x1[t].wait_recv()
        hb[t] = (sx[t, core] + rx[t]).astype(jnp.bfloat16)
        x2[t] = send(hb.at[t], hr.at[t], x2_send.at[t], x2_recv.at[t], across)

    def stage_g(t):
        x2[t].wait_recv()
        excess = hb[t].astype(jnp.float32) + hr[t].astype(jnp.float32) + MARGIN
        signed = sigma * OFFSET[t]
        order = 2 * abs(OFFSET[t]) - jnp.where(signed > 0, 1, 0)
        live = order * PB + col_half < tail_half
        if t == OWN:
            hot = col_half == pos_half
            live = live & jnp.logical_not(hot)
        e = jnp.exp(-jnp.abs(excess))
        soft = jnp.maximum(excess, 0.0) + jnp.log1p(e)
        sig = jnp.where(excess >= 0.0, 1.0, e) / (1.0 + e)
        state["loss"] += jnp.sum(jnp.where(live, soft, 0.0), axis=0, keepdims=True)
        g = jnp.where(live, sig * (LOSS_SCALE / count_half), 0.0)
        state["total"] += jnp.sum(g, axis=0, keepdims=True)
        if t == OWN:
            g = g - jnp.where(hot, state["total"], 0.0)
            lbuf[core] = jnp.broadcast_to(state["loss"] / count_half, (8, HALF))
            state["lossx"] = send(
                lbuf.at[core], lbuf.at[core], loss_send.at[0], loss_recv.at[0], mate
            )
        rows = pl.ds(t * PB, PB)
        gt[core, rows, :] = g.astype(jnp.bfloat16)
        x3[t] = send(
            gt.at[core, rows, :], gt.at[core, rows, :], x3_send.at[t], x3_recv.at[t], mate
        )

    def give_rows(t, value, to, rows, i):
        slot = t - 1
        ret_out[slot, rows, :] = value.astype(jnp.bfloat16)
        ret[t, i] = send(
            ret_out.at[slot, rows, :], ret_in.at[slot, rows, :],
            ret_send.at[slot, i], ret_recv.at[slot, i], dev(to),
        )

    def give(t, value, to, chunks):
        n = PB // chunks
        for i in range(chunks):
            give_rows(t, value[i * n:(i + 1) * n], to, pl.ds(i * n, n), i)

    def chain_n():
        n = PB // RC
        for i in range(RC):
            rows = pl.ds(i * n, n)
            ret[FAR, i].wait_recv()
            value = kpart[rows, :] + ret_in[FAR - 1, rows, :].astype(jnp.float32)
            give_rows(KR, value, K, rows, i)

    def chain_m():
        n = PB // RC
        ret[FR, 0].wait_recv()
        for i in range(RC):
            rows = pl.ds(i * n, n)
            ret[KR, i].wait_recv()
            value = rpart[rows, :] + ret_in[FR - 1, rows, :].astype(jnp.float32)
            value = value + ret_in[KR - 1, rows, :].astype(jnp.float32)
            give_rows(R, value, R, rows, i)

    def stage_d(t):
        x3[t].wait_recv()
        rows = pl.ds(t * PB, PB)
        part = jnp.dot(gt[0, rows, :], q[:HALF, :], preferred_element_type=jnp.float32)
        part = part + jnp.dot(gt[1, rows, :], q[HALF:, :], preferred_element_type=jnp.float32)
        part = part * SCALE
        if t == OWN:
            dp[...] = part
        elif t == R:
            rpart[...] = part
        elif t == KR and CHAIN:
            kpart[...] = part
        elif t == FAR:
            give(t, part, K if CHAIN else FAR, RC)
        elif t == KR:
            give(t, part, K, RC)
        else:
            give(t, part, F if t in (F, FR) else K, 1)
        prod = part * hpt[t].astype(jnp.float32)
        state["gain"] += jnp.sum(prod.reshape(PB // 8, 8, WIDTH), axis=0)

    out_copies = []

    def stage_q():
        for i in range(2):
            rows = pl.ds(i * HALF, HALF)
            dquery = lax.dot_general(
                gt[i], p[...], (((0,), (0,)), ((), ())), preferred_element_type=jnp.float32
            ) * SCALE
            dq[rows, :] = dquery * gain
            copy = pltpu.make_async_copy(dq.at[rows, :], gq_hbm.at[rows, :], out_sem.at[i])
            copy.start()
            out_copies.append(copy)
            prod = dquery * hq[rows, :].astype(jnp.float32)
            state["gain"] += jnp.sum(prod.reshape(HALF // 8, 8, WIDTH), axis=0)
        vec = jnp.sum(state["gain"], axis=0, keepdims=True)
        for i in range(8):
            zbuf[z, pl.ds(i, 1), :] = vec[:, i * 128:(i + 1) * 128]
        for k in range(1, NZ):
            z_copies.append(
                send(zbuf.at[z], zbuf.at[z], z_send.at[k - 1], z_recv.at[k - 1], z_peer(k))
            )

    z_copies, xy_copies = [], []

    def stage_z():
        for copy in z_copies:
            copy.wait_recv()
        line = zbuf[0]
        for i in range(1, NZ):
            line = line + zbuf[i]
        xbuf[place] = line
        for k in range(1, NXY):
            xy_copies.append(
                send(xbuf.at[place], xbuf.at[place], xy_send.at[k - 1], xy_recv.at[k - 1], xy_peer(k))
            )

    def stage_x():
        for copy in xy_copies:
            copy.wait_recv()
        plane = xbuf[0]
        for i in range(1, NXY):
            plane = plane + xbuf[i]
        gg_ref[...] = plane
        state["lossx"].wait_recv()
        loss_ref[...] = jnp.concatenate([lbuf[0, 0:1, :], lbuf[1, 0:1, :]], axis=1)

    stages = {
        "S": stage_s, "H": stage_h, "G": stage_g, "D": stage_d, "r": relay_r, "k": relay_k,
        "Q": stage_q, "Z": stage_z, "X": stage_x, "N": chain_n, "M": chain_m,
    }
    for step in ORDER:
        if step == "N" and not CHAIN:
            continue
        stages[step[0]](*[int(c) for c in step[1:]])

    total = dp[...]
    for t in (F, K, R) if CHAIN else (F, K, R, FAR):
        for i in range(1 if t in (F, K) else RC):
            ret[t, i].wait_recv()
        total = total + ret_in[t - 1].astype(jnp.float32)
    dp[...] = total * gain
    copy = pltpu.make_async_copy(dp, gp_hbm, out_sem.at[2])
    copy.start()
    out_copies.append(copy)
    for copy in sends:
        copy.wait_send()
    for copy in out_copies:
        copy.wait()


def shards(hidden_query, hidden_passage, embed_gain, positive, tail_count):
    vmem = pl.BlockSpec(memory_space=pltpu.VMEM)
    hbm = pl.BlockSpec(memory_space=pl.ANY)
    dma = pltpu.SemaphoreType.DMA
    gq, gp, gg, loss = pl.pallas_call(
        kernel,
        name="retrieval",
        out_shape=(
            jax.ShapeDtypeStruct((QB, WIDTH), jnp.float32),
            jax.ShapeDtypeStruct((PB, WIDTH), jnp.float32),
            jax.ShapeDtypeStruct((8, 128), jnp.float32),
            jax.ShapeDtypeStruct((1, QB), jnp.float32),
        ),
        in_specs=[hbm] * 5,
        out_specs=(hbm, hbm, vmem, vmem),
        scratch_shapes=[
            pltpu.VMEM((QB, WIDTH), jnp.bfloat16),
            pltpu.VMEM((1, WIDTH), jnp.float32),
            pltpu.VMEM((4, 128), jnp.int32),
            pltpu.VMEM((4, 128), jnp.int32),
            pltpu.VMEM((7, PB, WIDTH), jnp.bfloat16),
            pltpu.VMEM((QB, WIDTH), jnp.bfloat16),
            pltpu.VMEM((7 * PB, WIDTH), jnp.bfloat16),
            pltpu.VMEM((7, 2, PB, HALF), jnp.float32),
            pltpu.VMEM((7, PB, HALF), jnp.float32),
            pltpu.VMEM((7, PB, HALF), jnp.bfloat16),
            pltpu.VMEM((7, PB, HALF), jnp.bfloat16),
            pltpu.VMEM((2, 7 * PB, HALF), jnp.bfloat16),
            pltpu.VMEM((PB, WIDTH), jnp.float32),
            pltpu.VMEM((PB, WIDTH), jnp.float32),
            pltpu.VMEM((6, PB, WIDTH), jnp.bfloat16),
            pltpu.VMEM((6, PB, WIDTH), jnp.bfloat16),
            pltpu.VMEM((QB, WIDTH), jnp.float32),
            pltpu.VMEM((PB, WIDTH), jnp.float32),
            pltpu.VMEM((NZ, 8, 128), jnp.float32),
            pltpu.VMEM((NXY, 8, 128), jnp.float32),
            pltpu.VMEM((2, 8, HALF), jnp.float32),
            dma((5,)), dma((3,)), dma((7, FC)), dma((7, FC)), dma((7,)), dma((7,)), dma((7,)), dma((7,)),
            dma((7,)), dma((7,)), dma((6, RC)), dma((6, RC)), dma((NZ - 1,)), dma((NZ - 1,)),
            dma((NXY - 1,)), dma((NXY - 1,)), dma((1,)), dma((1,)),
        ],
        compiler_params=pltpu.CompilerParams(
            collective_id=0, has_side_effects=True, vmem_limit_bytes=60 * 1024 * 1024
        ),
    )(
        hidden_query, hidden_passage, embed_gain.reshape(1, WIDTH),
        positive.reshape(4, 128), tail_count.reshape(4, 128),
    )
    return gq, gp, gg.reshape(WIDTH), loss.reshape(QB)


def solution(mesh):
    in_specs = (P("blk", "feat"), P("blk", "feat"), P("feat"), P("blk"), P("blk"))
    out_specs = (P("blk", "feat"), P("blk", "feat"), P("feat"), P("blk"))
    return jax.shard_map(shards, mesh=mesh, in_specs=in_specs, out_specs=out_specs, check_vma=False)
```

time: 681 us -> 76.6 us (0.11)
  the two profiles are of different devices: /device:TPU:8 before, /device:TPU:1 now
where the time goes in v1:
time: 76.6 us; the launch traced here: 76.5 us
  Pallas kernels  70.6 us (92%)
  local copies, waits for them, and re-layouts  5.19 us (7%)
    pallas_call x1, Pallas kernels, shards(): pl.pallas_call(kernel, name='retrieval', out_shape=(jax.ShapeDtypeStruct(...  70.6 us
    unnamed x10, local copies, waits for them, and re-layouts  5.19 us

profile of v1, /device:TPU:1, one launch (start us, length us, event | category | flops | bytes accessed | tf_op | source)
XLA Modules:
  0.0 76.5 jit_solution(15826085108126910581)
XLA Ops:
  0.6 70.6 %retrieval.1 = (f32[512,1024]{1,0:T(8,128)}, f32[128,1024]{1,0:T(8,128)}, f32[8,128]{1,0:T(8,128)}, f32[1,512]{1,0:T(1,128)}) custom-call(bf16[512,1024]{1,0:T(8,128)(2,1)} %hq_hbm.1, bf16[128,1024]{1,0:T(8,128)(2,1)} %hp_hbm.1, f32[1,1024]{1,0:T(1,128)} %bitcast.5, s32[4,128]{1,0:T(4,128)} %bitcast.7, s32[4,128]{1,0:T(4,128)} %bitcast.8), custom_call_target="tpu_custom_call" | custom-call | tf_op jit(solution)/shard_map/retrieval/pallas_call | solution.py:317
  71.3 0.0 copy-start
  71.3 0.0 copy-start.1
  71.3 0.0 copy-start.2
  71.3 3.2 %copy.13 = f32[512,1024]{1,0:T(8,128)} copy(f32[512,1024]{1,0:T(8,128)} %get-tuple-element.16) | data formatting | bytes 4194304
  74.5 0.0 copy-done
  74.5 0.8 %copy.14 = f32[128,1024]{1,0:T(8,128)} copy(f32[128,1024]{1,0:T(8,128)S(1)} %copy-done) | data formatting | bytes 1048576
  75.3 0.0 copy-done.1
  75.3 0.6 copy.15
  75.9 0.0 copy-done.2
  75.9 0.6 copy.16
Async XLA Ops:
  71.3 3.2 %copy-start = (f32[128,1024]{1,0:T(8,128)S(1)}, f32[128,1024]{1,0:T(8,128)}, u32[]{:S(2)}) copy-start(f32[128,1024]{1,0:T(8,128)} %get-tuple-element.17) | copy-start | bytes 1572868
  71.3 4.0 %copy-start.1 = (f32[8,128]{1,0:T(8,128)S(1)}, f32[8,128]{1,0:T(8,128)}, u32[]{:S(2)}) copy-start(f32[8,128]{1,0:T(8,128)} %get-tuple-element.10) | copy-start | bytes 12292
  71.3 4.6 %copy-start.2 = (f32[1,512]{1,0:T(1,128)S(1)}, f32[1,512]{1,0:T(1,128)}, u32[]{:S(2)}) copy-start(f32[1,512]{1,0:T(1,128)} %get-tuple-element.11) | copy-start | bytes 6148

commit v2 on v1

--- a/solution.py
+++ b/solution.py
@@ -23,21 +23,25 @@
 ROLES = (R, F, K, FR, KR, FAR)
 
 ORDER = (
-    "S0", "r0", "H0", "r1", "S1", "S2", "H1", "S3", "H2", "H3", "k0", "G1", "G2", "k1", "S5", "G3",
-    "D2", "D3", "S4", "H5", "H4", "D1", "S6", "G5", "G4", "H6", "D5", "D4", "G6", "G0",
-    "D6", "D0", "Q", "N", "M", "Z", "X",
+    "S0", "r0", "f0", "r1", "f1", "H0", "r2", "f2", "r3", "f3", "S1", "S2", "H1", "S3", "k0", "H2", "k1",
+    "H3", "G1", "k2", "G2", "k3", "S5", "B", "G3", "S4", "H5", "D3", "H4", "D1", "S6", "G5", "H6",
+    "G4", "D5", "D4", "D2", "L", "G6", "G0", "D6", "D0", "Q", "N", "M", "Z", "X",
 )
-FC = 2
+FC = 4
+VM1 = 60
+VM2 = 62
+FWD_RUNG = True
+RET_RUNG = False
 RC = 4
-CHAIN = True
+RL = 1
 
 
 def kernel(
     hq_hbm, hp_hbm, gain_hbm, pos_hbm, tail_hbm,
     gq_hbm, gp_hbm, gg_ref, loss_ref,
-    hq, gain_ref, pos_ref, tail_ref, hpt, q, p, sx, rx, hb, hr, gt, rpart, kpart, ret_out, ret_in, dq, dp, zbuf, xbuf, lbuf,
+    hq, gain_ref, pos_ref, tail_ref, hpt, q, p, sx, rx, hb, hr, gt, rpart, fpart, kpart, ret_out, ret_in, dq, dp, zbuf, xbuf, lbuf,
     local_sem, out_sem, fwd_send, fwd_recv, x1_send, x1_recv, x2_send, x2_recv,
-    x3_send, x3_recv, ret_send, ret_recv, z_send, z_recv, xy_send, xy_recv, loss_send, loss_recv,
+    x3_send, x3_recv, ret_send, ret_recv, z_send, z_recv, xy_send, xy_recv, loss_send, loss_recv, known,
 ):
     b = lax.axis_index("blk")
     f = lax.axis_index("feat")
@@ -77,11 +81,28 @@
         copy.start()
 
     peers = [dev(r) for r in ROLES] + [mate, across]
-    peers += [z_peer(k) for k in range(1, NZ)] + [xy_peer(k) for k in range(1, NXY)]
+    peers += [z_peer(k) for k in (1, 2, 3, NZ - 3, NZ - 2, NZ - 1)]
+    peers += [xy_peer(k) for k in range(1, NXY)]
     barrier = pltpu.get_barrier_semaphore()
     for peer in peers:
         pl.semaphore_signal(barrier, inc=1, device_id=peer, device_id_type=MESH)
     pl.semaphore_wait(barrier, len(peers))
+
+    def tell(i, steps):
+        for side, k in enumerate((steps, NZ - steps)):
+            pl.semaphore_signal(
+                known.at[i, side], inc=1, device_id=z_peer(k), device_id_type=MESH
+            )
+
+    def heard(i):
+        for side in range(2):
+            pl.semaphore_wait(known.at[i, side], 1)
+
+    tell(0, 3)
+
+    def stage_b():
+        heard(0)
+        tell(1, 2)
 
     sends = []
 
@@ -131,15 +152,21 @@
 
     def relay_r(i):
         fwd[R, i].wait_recv()
-        fwd[KR, i] = forward(hpt.at[R], KR, i, F)
+        if not FWD_RUNG:
+            fwd[KR, i] = forward(hpt.at[R], KR, i, F)
         fwd[FR, i] = forward(hpt.at[R], FR, i, K)
+
+    def relay_f(i):
+        fwd[F, i].wait_recv()
+        if FWD_RUNG:
+            fwd[KR, i] = forward(hpt.at[F], KR, i, R)
 
     def relay_k(i):
         fwd[KR, i].wait_recv()
         fwd[FAR, i] = forward(hpt.at[KR], FAR, i, F)
 
     def stage_s(t):
-        if t in (F, K, FR, FAR):
+        if t in (K, FR, FAR):
             for i in range(FC):
                 fwd[t, i].wait_recv()
         rows = pl.ds(t * PB, PB)
@@ -201,23 +228,31 @@
         for i in range(chunks):
             give_rows(t, value[i * n:(i + 1) * n], to, pl.ds(i * n, n), i)
 
+    def add_on(t, part, after, to, chunks):
+        n = PB // chunks
+        for i in range(chunks):
+            rows = pl.ds(i * n, n)
+            value = part[rows, :]
+            for other in after:
+                ret[other, i].wait_recv()
+                value = value + ret_in[other - 1, rows, :].astype(jnp.float32)
+            give_rows(t, value, to, rows, i)
+
+    def chain_l():
+        if RET_RUNG:
+            add_on(R, rpart, (FR,), R, RL)
+
     def chain_n():
-        n = PB // RC
-        for i in range(RC):
-            rows = pl.ds(i * n, n)
-            ret[FAR, i].wait_recv()
-            value = kpart[rows, :] + ret_in[FAR - 1, rows, :].astype(jnp.float32)
-            give_rows(KR, value, K, rows, i)
+        add_on(KR, kpart, (FAR,), R if RET_RUNG else K, RC)
 
     def chain_m():
-        n = PB // RC
-        ret[FR, 0].wait_recv()
-        for i in range(RC):
-            rows = pl.ds(i * n, n)
-            ret[KR, i].wait_recv()
-            value = rpart[rows, :] + ret_in[FR - 1, rows, :].astype(jnp.float32)
-            value = value + ret_in[KR - 1, rows, :].astype(jnp.float32)
-            give_rows(R, value, R, rows, i)
+        if RET_RUNG:
+            add_on(F, fpart, (KR,), F, RC)
+        else:
+            add_on(R, rpart, (FR, KR), R, RC)
+
+    pieces = {K: 1, F: RC if RET_RUNG else 1, FR: RL if RET_RUNG else RC, R: RL if RET_RUNG else RC}
+    held = {R: rpart, F: fpart, KR: kpart} if RET_RUNG else {R: rpart, KR: kpart}
 
     def stage_d(t):
         x3[t].wait_recv()
@@ -227,16 +262,12 @@
         part = part * SCALE
         if t == OWN:
             dp[...] = part
-        elif t == R:
-            rpart[...] = part
-        elif t == KR and CHAIN:
-            kpart[...] = part
+        elif t in held:
+            held[t][...] = part
         elif t == FAR:
-            give(t, part, K if CHAIN else FAR, RC)
-        elif t == KR:
             give(t, part, K, RC)
         else:
-            give(t, part, F if t in (F, FR) else K, 1)
+            give(t, part, K if t == K else F, pieces[t])
         prod = part * hpt[t].astype(jnp.float32)
         state["gain"] += jnp.sum(prod.reshape(PB // 8, 8, WIDTH), axis=0)
 
@@ -257,6 +288,7 @@
         vec = jnp.sum(state["gain"], axis=0, keepdims=True)
         for i in range(8):
             zbuf[z, pl.ds(i, 1), :] = vec[:, i * 128:(i + 1) * 128]
+        heard(1)
         for k in range(1, NZ):
             z_copies.append(
                 send(zbuf.at[z], zbuf.at[z], z_send.at[k - 1], z_recv.at[k - 1], z_peer(k))
@@ -289,15 +321,14 @@
     stages = {
         "S": stage_s, "H": stage_h, "G": stage_g, "D": stage_d, "r": relay_r, "k": relay_k,
         "Q": stage_q, "Z": stage_z, "X": stage_x, "N": chain_n, "M": chain_m,
+        "L": chain_l, "f": relay_f, "B": stage_b,
     }
     for step in ORDER:
-        if step == "N" and not CHAIN:
-            continue
         stages[step[0]](*[int(c) for c in step[1:]])
 
     total = dp[...]
-    for t in (F, K, R) if CHAIN else (F, K, R, FAR):
-        for i in range(1 if t in (F, K) else RC):
+    for t in (K, R, F):
+        for i in range(pieces[t]):
             ret[t, i].wait_recv()
         total = total + ret_in[t - 1].astype(jnp.float32)
     dp[...] = total * gain
@@ -308,6 +339,23 @@
         copy.wait_send()
     for copy in out_copies:
         copy.wait()
+
+
+def finish(*refs):
+    sources, results, held, sem_in, sem_out = refs[:4], refs[4:8], refs[8:12], refs[12], refs[13]
+    parts = [(i, slice(None)) for i in (1, 2, 3)]
+    parts += [(0, pl.ds(j * (QB // 4), QB // 4)) for j in range(4)]
+    copies = []
+    for n, (i, rows) in enumerate(parts):
+        into = pltpu.make_async_copy(sources[i].at[rows], held[i].at[rows], sem_in.at[n])
+        out = pltpu.make_async_copy(held[i].at[rows], results[i].at[rows], sem_out.at[n])
+        into.start()
+        copies.append((into, out))
+    for into, out in copies:
+        into.wait()
+        out.start()
+    for _, out in copies:
+        out.wait()
 
 
 def shards(hidden_query, hidden_passage, embed_gain, positive, tail_count):
@@ -340,6 +388,7 @@
             pltpu.VMEM((2, 7 * PB, HALF), jnp.bfloat16),
             pltpu.VMEM((PB, WIDTH), jnp.float32),
             pltpu.VMEM((PB, WIDTH), jnp.float32),
+            pltpu.VMEM((PB, WIDTH), jnp.float32),
             pltpu.VMEM((6, PB, WIDTH), jnp.bfloat16),
             pltpu.VMEM((6, PB, WIDTH), jnp.bfloat16),
             pltpu.VMEM((QB, WIDTH), jnp.float32),
@@ -350,14 +399,25 @@
             dma((5,)), dma((3,)), dma((7, FC)), dma((7, FC)), dma((7,)), dma((7,)), dma((7,)), dma((7,)),
             dma((7,)), dma((7,)), dma((6, RC)), dma((6, RC)), dma((NZ - 1,)), dma((NZ - 1,)),
             dma((NXY - 1,)), dma((NXY - 1,)), dma((1,)), dma((1,)),
+            pltpu.SemaphoreType.REGULAR((2, 2)),
         ],
         compiler_params=pltpu.CompilerParams(
-            collective_id=0, has_side_effects=True, vmem_limit_bytes=60 * 1024 * 1024
+            collective_id=0, has_side_effects=True, vmem_limit_bytes=VM1 * 1024 * 1024
         ),
     )(
         hidden_query, hidden_passage, embed_gain.reshape(1, WIDTH),
         positive.reshape(4, 128), tail_count.reshape(4, 128),
     )
+    outs = (gq, gp, gg, loss)
+    gq, gp, gg, loss = pl.pallas_call(
+        finish,
+        name="finish",
+        out_shape=tuple(jax.ShapeDtypeStruct(o.shape, o.dtype) for o in outs),
+        in_specs=[hbm] * 4,
+        out_specs=(hbm,) * 4,
+        scratch_shapes=[pltpu.VMEM(o.shape, o.dtype) for o in outs] + [dma((7,)), dma((7,))],
+        compiler_params=pltpu.CompilerParams(vmem_limit_bytes=VM2 * 1024 * 1024),
+    )(*outs)
     return gq, gp, gg.reshape(WIDTH), loss.reshape(QB)
 
 

time: 76.6 us -> 71.7 us (0.936)
  local copies, waits for them, and re-layouts: 5.19 us -> 0 us
    unnamed x10 -> x0, local copies, waits for them, and re-layouts: 5.19 us -> none
    pallas_call x0 -> x1, Pallas kernels: none -> 2.66 us  [shards(): pl.pallas_call(finish, name='finish', out_shape=tuple((jax.ShapeDtypeStru...]
    pallas_call x1, Pallas kernels: 70.6 us -> 68.2 us  [shards(): pl.pallas_call(kernel, name='retrieval', out_shape=(jax.ShapeDtypeStruct(...]
where the time goes in v2:
time: 71.7 us; the launch traced here: 71.5 us
  Pallas kernels  70.9 us (99%)
    pallas_call x1, Pallas kernels, shards(): pl.pallas_call(kernel, name='retrieval', out_shape=(jax.ShapeDtypeStruct(...  68.2 us
    pallas_call x1, Pallas kernels, shards(): pl.pallas_call(finish, name='finish', out_shape=tuple((jax.ShapeDtypeStru...  2.66 us

profile of v2, /device:TPU:1, one launch (start us, length us, event | category | flops | bytes accessed | tf_op | source)
XLA Modules:
  0.0 71.5 jit_solution(2491014530381944762)
XLA Ops:
  0.6 68.2 %retrieval.1 = (f32[512,1024]{1,0:T(8,128)}, f32[128,1024]{1,0:T(8,128)}, f32[8,128]{1,0:T(8,128)}, f32[1,512]{1,0:T(1,128)}) custom-call(bf16[512,1024]{1,0:T(8,128)(2,1)} %hq_hbm.1, bf16[128,1024]{1,0:T(8,128)(2,1)} %hp_hbm.1, f32[1,1024]{1,0:T(1,128)} %bitcast.5, s32[4,128]{1,0:T(4,128)} %bitcast.6, s32[4,128]{1,0:T(4,128)} %bitcast.7), custom_call_target="tpu_custom_call" | custom-call | tf_op jit(solution)/shard_map/retrieval/pallas_call | solution.py:365
  68.9 2.7 %finish.1 = (f32[512,1024]{1,0:T(8,128)}, f32[128,1024]{1,0:T(8,128)}, f32[8,128]{1,0:T(8,128)}, f32[1,512]{1,0:T(1,128)}) custom-call(f32[512,1024]{1,0:T(8,128)} %get-tuple-element.12.refs_0_, f32[128,1024]{1,0:T(8,128)} %get-tuple-element.13.refs_1_, f32[8,128]{1,0:T(8,128)} %get-tuple-element.14.refs_2_, f32[1,512]{1,0:T(1,128)} %get-tuple-element.15.refs_3_), custom_call_target="tpu_custom_call" | custom-call | tf_op jit(solution)/shard_map/finish/pallas_call | solution.py:412

commit v3 on v2

--- a/solution.py
+++ b/solution.py
@@ -124,7 +124,6 @@
     fwd = {}
     for i in range(FC):
         fwd[R, i] = forward(hp_hbm, R, i, R)
-    for i in range(FC):
         fwd[K, i] = forward(hp_hbm, K, i, F)
         fwd[F, i] = forward(hp_hbm, F, i, K)
 
@@ -289,7 +288,7 @@
         for i in range(8):
             zbuf[z, pl.ds(i, 1), :] = vec[:, i * 128:(i + 1) * 128]
         heard(1)
-        for k in range(1, NZ):
+        for k in sorted(range(1, NZ), key=lambda k: abs(k - NZ // 2)):
             z_copies.append(
                 send(zbuf.at[z], zbuf.at[z], z_send.at[k - 1], z_recv.at[k - 1], z_peer(k))
             )

time: 71.7 us -> 71.7 us (level)
  no operation moved by 1% of the time
where the time goes in v3:
time: 71.7 us; the launch traced here: 71.5 us
  Pallas kernels  70.9 us (99%)
    pallas_call x1, Pallas kernels, shards(): pl.pallas_call(kernel, name='retrieval', out_shape=(jax.ShapeDtypeStruct(...  68.2 us
    pallas_call x1, Pallas kernels, shards(): pl.pallas_call(finish, name='finish', out_shape=tuple((jax.ShapeDtypeStru...  2.66 us

profile of v3, /device:TPU:1, one launch (start us, length us, event | category | flops | bytes accessed | tf_op | source)
XLA Modules:
  0.0 71.5 jit_solution(8805484532672017801)
XLA Ops:
  0.6 68.2 %retrieval.1 = (f32[512,1024]{1,0:T(8,128)}, f32[128,1024]{1,0:T(8,128)}, f32[8,128]{1,0:T(8,128)}, f32[1,512]{1,0:T(1,128)}) custom-call(bf16[512,1024]{1,0:T(8,128)(2,1)} %hq_hbm.1, bf16[128,1024]{1,0:T(8,128)(2,1)} %hp_hbm.1, f32[1,1024]{1,0:T(1,128)} %bitcast.5, s32[4,128]{1,0:T(4,128)} %bitcast.6, s32[4,128]{1,0:T(4,128)} %bitcast.7), custom_call_target="tpu_custom_call" | custom-call | tf_op jit(solution)/shard_map/retrieval/pallas_call | solution.py:364
  68.9 2.7 %finish.1 = (f32[512,1024]{1,0:T(8,128)}, f32[128,1024]{1,0:T(8,128)}, f32[8,128]{1,0:T(8,128)}, f32[1,512]{1,0:T(1,128)}) custom-call(f32[512,1024]{1,0:T(8,128)} %get-tuple-element.12.refs_0_, f32[128,1024]{1,0:T(8,128)} %get-tuple-element.13.refs_1_, f32[8,128]{1,0:T(8,128)} %get-tuple-element.14.refs_2_, f32[1,512]{1,0:T(1,128)} %get-tuple-element.15.refs_3_), custom_call_target="tpu_custom_call" | custom-call | tf_op jit(solution)/shard_map/finish/pallas_call | solution.py:411
